TPU v7x, 256 devices: a whole 4x4x8 slice. The times are simulated.
256 devices in a mesh: row: 32 (over y, x, core), col: 8 (over z).
Axes of the slice: x: 4, y: 4, z: 8, core: 2. Of those that a mesh axis runs over, the one named last changes fastest.
Arguments:
- start: float32 [65536, 128], P(('row', 'col')), may hold values from -6 to 6
- tiles: float32 [256, 24, 256, 256], P(('row', 'col')), may hold values from -0.375 to 0.375
- tile_rows: int32 [256, 24], P(('row', 'col')), may hold values from 0 to 7, as said below
- tile_cols: int32 [256, 24], P(('row', 'col')), may hold values from 0 to 31, as said below
- tile_count: int32 [256], P(('row', 'col')), may hold values from 1 to 24, as said below
Outputs:
- basis: float32 [65536, 128], P(('row', 'col'))
- factor: float32 [128, 128], replicated
Inputs may be any that keep to these rules, and one draw needn't show every extreme that they name: Within the first tile_count[d] slots of a device the pairs (tile_rows, tile_cols) are distinct; later slots may hold anything in range. `tile_cols`: see tile_rows. `tile_count`: counts differ from device to device; some device is full.
All inputs are finite; a program needn't handle non-finite values.
Results may differ from a plain program's by a relative error of at most 0.0003.
Values sent between devices are 32-bit elements; how exact they have to be, the bound alone decides.
A program may use at most 64 MiB of HBM per device.

v0:
```python
import jax
import jax.numpy as jnp
from jax import lax
from jax.sharding import PartitionSpec as P

ITERS = 2


def solve_rows(factor, block):
    return jax.scipy.linalg.solve_triangular(factor, block.T, lower=True).T


def spread(vectors):
    near = lax.all_gather(vectors, "col", axis=0, tiled=True)
    far = lax.all_gather(vectors, "row", axis=0, tiled=True)
    return (near, far)


def products(near, far, tiles, tile_rows, tile_cols, tile_count):
    width = near.shape[1]
    size = tiles.shape[2]
    near_blocks = near.reshape(-1, size, width)
    far_blocks = far.reshape(-1, size, width)
    n_near = near_blocks.shape[0]
    n_far = far_blocks.shape[0]
    pieces = tiles[0]
    rows = tile_rows[0]
    cols = tile_cols[0]
    count = tile_count[0]
    live = (jnp.arange(pieces.shape[0], dtype=jnp.int32) < count).astype(jnp.float32)
    upper = jnp.einsum("kpq,kqf->kpf", pieces, far_blocks[cols], precision=lax.Precision.HIGHEST)
    mirror = jnp.einsum("kqp,kqf->kpf", pieces, near_blocks[rows], precision=lax.Precision.HIGHEST)
    pick_near = (rows[:, None] == jnp.arange(n_near, dtype=jnp.int32)[None, :]).astype(
        jnp.float32
    ) * live[:, None]
    pick_far = (cols[:, None] == jnp.arange(n_far, dtype=jnp.int32)[None, :]).astype(
        jnp.float32
    ) * live[:, None]
    near_out = jnp.einsum("ka,kpf->apf", pick_near, upper, precision=lax.Precision.HIGHEST)
    far_out = jnp.einsum("kb,kpf->bpf", pick_far, mirror, precision=lax.Precision.HIGHEST)
    return (near_out.reshape(-1, width), far_out.reshape(-1, width))


def shards(start, tiles, tile_rows, tile_cols, tile_count):
    total_nodes = lax.axis_size("row") * lax.axis_size("col") * start.shape[0]
    basis = start
    image = start
    factor = jnp.zeros((start.shape[1], start.shape[1]), jnp.float32)
    for step in range(ITERS):
        near, far = spread(basis)
        near_part, far_part = products(near, far, tiles, tile_rows, tile_cols, tile_count)
        image = lax.psum_scatter(
            near_part, "col", scatter_dimension=0, tiled=True
        ) + lax.psum_scatter(far_part, "row", scatter_dimension=0, tiled=True)
        local_gram = jnp.dot(
            image.T, image, precision=lax.Precision.HIGHEST, preferred_element_type=jnp.float32
        )
        gram = lax.psum(local_gram, ("row", "col")) / total_nodes
        factor = jnp.linalg.cholesky(gram)
        basis = solve_rows(factor, image)
    return (basis, factor)


def solution(mesh):
    placed = (
        P(("row", "col"), None),
        P(("row", "col"), None, None, None),
        P(("row", "col"), None),
        P(("row", "col"), None),
        P(("row", "col")),
    )
    return jax.shard_map(
        shards,
        mesh=mesh,
        in_specs=placed,
        out_specs=(P(("row", "col"), None), P()),
        check_vma=False,
    )
```

profile of v0, /device:TPU:1, one launch (start us, length us, event | category | flops | bytes accessed | tf_op | source)
XLA Modules:
  0.0 1010.7 jit_solution(1625149289480719164)
XLA Ops:
  7.2 0.7 all-gather.7.cloned.1.call-update
  7.9 0.0 all-gather.5.cloned.1.call-start
  7.9 0.7 all-gather.5.cloned.1.call-update
  8.6 0.0 reduce-scatter.7.cloned.1.call-start
  9.3 0.7 fusion.53
  10.0 37.2 %all-gather.7.cloned.1.call-done = f32[2048,128]{1,0:T(8,128)} async-done(((f32[256,128]{1,0:T(8,128)}), f32[2048,128]{1,0:T(8,128)}) %all-gather.7.cloned.1.call-update) | async-done | bytes 1048592 | tf_op jit(solution)/shard_map/all_gather | solution.py:14
  47.2 2.0 gather_fusion.1
  49.2 9.7 fusion.4
  59.0 3.0 copy.24
  62.0 3.6 fusion.12
  65.6 4.4 copy.13
  70.0 0.2 reduce-scatter.5.cloned.1.call-start
  70.3 34.6 %all-gather.5.cloned.1.call-done = f32[8192,128]{1,0:T(8,128)} async-done(((f32[256,128]{1,0:T(8,128)}), f32[8192,128]{1,0:T(8,128)}) %all-gather.5.cloned.1.call-update) | async-done | bytes 4194320 | tf_op jit(solution)/shard_map/all_gather | solution.py:15
  104.9 2.9 gather_fusion
  107.9 11.1 %fusion.6 = f32[24,128,256]{2,1,0:T(8,128)} fusion(f32[24,256,128]{2,1,0:T(8,128)S(1)} %gather_fusion, f32[1,24,256,256]{3,2,1,0:T(8,128)} %param.9), kind=kOutput, calls=%fused_computation.10 | convolution fusion | flops 2415919104 | bytes 12582912 | tf_op jit(solution)/shard_map/kpq,kqf->kpf/dot_general | solution.py:31
  119.0 2.5 copy.23
  121.5 1.6 fusion.14
  123.2 1.2 copy.12
  124.4 0.0 all-reduce.3.cloned.1.call-start
  124.4 71.4 %reduce-scatter.7.cloned.1.call-done = f32[256,128]{1,0:T(8,128)} async-done(((f32[8192,128]{1,0:T(8,128)}), f32[256,128]{1,0:T(8,128)}) %reduce-scatter.7.cloned.1.call-update) | async-done | bytes 131088 | tf_op jit(solution)/shard_map/reduce_scatter | solution.py:54
  195.8 37.4 %reduce-scatter.5.cloned.1.call-done = f32[256,128]{1,0:T(8,128)} async-done(((f32[2048,128]{1,0:T(8,128)}), f32[256,128]{1,0:T(8,128)}) %reduce-scatter.5.cloned.1.call-update) | async-done | bytes 131088 | tf_op jit(solution)/shard_map/reduce_scatter | solution.py:52
  233.2 2.1 fusion.30
  235.4 0.3 all-gather.11.cloned.1.call-start
  235.6 246.0 %all-reduce.3.cloned.1.call-done = f32[128,128]{0,1:T(8,128)} async-done(((f32[128,128]{0,1:T(8,128)}), f32[128,128]{0,1:T(8,128)}) %all-reduce.3.cloned.1.call-update) | async-done | bytes 65552 | tf_op jit(solution)/shard_map/psum | solution.py:58
  481.7 0.8 broadcast_multiply_fusion.1
  482.5 0.1 copy.15
  482.6 0.9 fusion.22
  483.5 11.7 %cholesky.44 = f32[128,128]{1,0:T(8,128)S(1)} custom-call(f32[128,128]{1,0:T(8,128)S(1)} %fusion.22), custom_call_target="Cholesky" | custom-call | tf_op jit(solution)/shard_map/jit(cholesky)/cholesky | solution.py:59
  495.2 0.6 compare_reduce_fusion.1
  495.8 0.7 fusion.18
  496.5 9.8 custom-call.6
  506.3 1.9 convolution_bitcast_fusion.1
  508.3 0.0 all-gather.9.cloned.1.call-start
  508.3 0.7 all-gather.9.cloned.1.call-update
  509.0 0.3 reduce-scatter.11.cloned.1.call-start
  509.3 28.8 %all-gather.11.cloned.1.call-done = f32[2048,128]{0,1:T(8,128)} async-done(((f32[256,128]{0,1:T(8,128)}), f32[2048,128]{0,1:T(8,128)}) %all-gather.11.cloned.1.call-update) | async-done | bytes 1048592 | tf_op jit(solution)/shard_map/all_gather | solution.py:14
  538.1 1.5 copy.30
  539.7 2.4 gather_fusion.3
  542.1 9.0 fusion
  551.2 2.8 copy.27
  554.0 5.5 fusion.8
  559.5 4.4 copy.19
  563.9 0.0 reduce-scatter.9.cloned.1.call-start
  563.9 35.7 %all-gather.9.cloned.1.call-done = f32[8192,128]{0,1:T(8,128)} async-done(((f32[256,128]{0,1:T(8,128)}), f32[8192,128]{0,1:T(8,128)}) %all-gather.9.cloned.1.call-update) | async-done | bytes 4194320 | tf_op jit(solution)/shard_map/all_gather | solution.py:15
  599.6 5.7 copy.29
  605.4 2.9 gather_fusion.2
  608.3 11.1 %fusion.2 = f32[24,128,256]{2,1,0:T(8,128)} fusion(f32[24,256,128]{2,1,0:T(8,128)S(1)} %gather_fusion.2, f32[1,24,256,256]{3,2,1,0:T(8,128)} %param.9), kind=kOutput, calls=%fused_computation.6 | convolution fusion | flops 2415919104 | bytes 12582912 | tf_op jit(solution)/shard_map/kpq,kqf->kpf/dot_general | solution.py:31
  619.4 2.6 copy.26
  622.0 1.6 fusion.10
  623.6 1.2 copy.17
  624.8 0.3 all-reduce.5.cloned.1.call-start
  625.1 66.2 %reduce-scatter.11.cloned.1.call-done = f32[256,128]{1,0:T(8,128)} async-done(((f32[8192,128]{1,0:T(8,128)}), f32[256,128]{1,0:T(8,128)}) %reduce-scatter.11.cloned.1.call-update) | async-done | bytes 131088 | tf_op jit(solution)/shard_map/reduce_scatter | solution.py:54
  691.2 37.4 %reduce-scatter.9.cloned.1.call-done = f32[256,128]{1,0:T(8,128)} async-done(((f32[2048,128]{1,0:T(8,128)}), f32[256,128]{1,0:T(8,128)}) %reduce-scatter.9.cloned.1.call-update) | async-done | bytes 131088 | tf_op jit(solution)/shard_map/reduce_scatter | solution.py:52
  728.6 2.1 fusion.27
  730.7 245.5 %all-reduce.5.cloned.1.call-done = f32[128,128]{0,1:T(8,128)} async-done(((f32[128,128]{0,1:T(8,128)}), f32[128,128]{0,1:T(8,128)}) %all-reduce.5.cloned.1.call-update) | async-done | bytes 65552 | tf_op jit(solution)/shard_map/psum | solution.py:58
  976.3 0.8 broadcast_multiply_fusion
  977.1 0.1 copy.21
  977.2 0.9 fusion.20
  978.1 11.7 %cholesky.55 = f32[128,128]{1,0:T(8,128)S(1)} custom-call(f32[128,128]{1,0:T(8,128)S(1)} %fusion.20), custom_call_target="Cholesky" | custom-call | tf_op jit(solution)/shard_map/jit(cholesky)/cholesky | solution.py:59
  989.8 0.6 compare_reduce_fusion
  990.5 1.3 select_bitcast_fusion
  991.7 9.8 custom-call.7
  1001.6 1.3 convolution_bitcast_fusion
  1002.8 0.8 copy.22
  (18 shorter events, 0.3 us)
Async XLA Ops:
  7.2 40.1 %all-gather.7.cloned.1.call-start = ((), (), s32[]{:S(2)}) async-start(), calls=%async_computation.6 | async-start | bytes 1179648 | tf_op jit(solution)/shard_map/all_gather | solution.py:14
  7.9 97.0 %all-gather.5.cloned.1.call-start = ((), (), s32[]{:S(2)}) async-start(), calls=%async_computation.4 | async-start | bytes 4325376 | tf_op jit(solution)/shard_map/all_gather | solution.py:15
  8.6 187.2 %reduce-scatter.7.cloned.1.call-start = ((), (), s32[]{:S(2)}) async-start(), calls=%async_computation.7 | async-start | bytes 4325376 | tf_op jit(solution)/shard_map/reduce_scatter | solution.py:54
  59.0 3.1 copy-start
  70.0 163.2 %reduce-scatter.5.cloned.1.call-start = ((), (), s32[]{:S(2)}) async-start(), calls=%async_computation.5 | async-start | bytes 1179648 | tf_op jit(solution)/shard_map/reduce_scatter | solution.py:52
  119.0 2.6 copy-start.1
  124.4 357.3 %all-reduce.3.cloned.1.call-start = ((), (), s32[]{:S(2)}) async-start(), calls=%async_computation.8 | async-start | bytes 131072 | tf_op jit(solution)/shard_map/psum | solution.py:58
  235.4 302.8 %all-gather.11.cloned.1.call-start = ((), (), s32[]{:S(2)}) async-start(), calls=%async_computation.11 | async-start | bytes 1179648 | tf_op jit(solution)/shard_map/all_gather | solution.py:14
  508.3 91.4 %all-gather.9.cloned.1.call-start = ((), (), s32[]{:S(2)}) async-start(), calls=%async_computation.9 | async-start | bytes 4325376 | tf_op jit(solution)/shard_map/all_gather | solution.py:15
  509.0 182.2 %reduce-scatter.11.cloned.1.call-start = ((), (), s32[]{:S(2)}) async-start(), calls=%async_computation.12 | async-start | bytes 4325376 | tf_op jit(solution)/shard_map/reduce_scatter | solution.py:54
  563.9 164.7 %reduce-scatter.9.cloned.1.call-start = ((), (), s32[]{:S(2)}) async-start(), calls=%async_computation.10 | async-start | bytes 1179648 | tf_op jit(solution)/shard_map/reduce_scatter | solution.py:52
  624.8 351.5 %all-reduce.5.cloned.1.call-start = ((), (), s32[]{:S(2)}) async-start(), calls=%async_computation.13 | async-start | bytes 131072 | tf_op jit(solution)/shard_map/psum | solution.py:58
Sparse Core Ops, SparseCore 0:
  9.8 37.4 all-gather.6
  49.8 55.0 all-gather.4
  108.9 86.9 reduce-scatter.6
  198.4 34.7 reduce-scatter.4
  240.0 241.5 all-reduce.2
  508.4 29.6 all-gather.10
  541.5 58.1 all-gather.8
  604.1 87.0 reduce-scatter.10
  693.8 34.7 reduce-scatter.8
  734.5 241.6 all-reduce.4
where the time goes:
time: 1020 us; the launch traced here: 1010 us
  waiting for transfers between devices  842 us (83%)
  matrix products  60.7 us (6%)
  other arithmetic  50.4 us (5%)
  local copies, waits for them, and re-layouts  40.6 us (4%)
  between operations  15.2 us (1%)
    psum x2, waiting for transfers between devices, shards(): gram = lax.psum(local_gram, ('row', 'col')) / total_nodes  492 us
    reduce_scatter x2, waiting for transfers between devices, shards(): lax.psum_scatter(far_part, 'row', scatter_dimension=0, tiled=True)  138 us
    reduce_scatter x2, waiting for transfers between devices, shards(): lax.psum_scatter(near_part, 'col', scatter_dimension=0, tiled=True)  74.7 us
    all_gather x2, waiting for transfers between devices, spread(): far = lax.all_gather(vectors, 'row', axis=0, tiled=True)  70.3 us
    all_gather x2, waiting for transfers between devices, spread(): near = lax.all_gather(vectors, 'col', axis=0, tiled=True)  66 us
    another operation x6, other arithmetic, shards(): factor = jnp.linalg.cholesky(gram)  24.8 us
    dot_general x2, matrix products, products(): jnp.einsum('kpq,kqf->kpf', pieces, far_blocks[cols], precision=lax.Precis...  22.2 us
    another operation x4, other arithmetic, solve_rows(): return jax.scipy.linalg.solve_triangular(factor, block.T, lower=True).T  21.6 us
  transfers between devices with their start and end apart: 10, of which 10 were waited for; matrix products, arithmetic and copies ran while one was open for 9% of the time, Pallas kernels for 0%

commit v1 on v0

v1 whole, which is shorter than its diff:
```python
from types import SimpleNamespace

import jax
import jax.numpy as jnp
from jax import lax
from jax.experimental import pallas as pl
from jax.experimental.pallas import tpu as pltpu
from jax.sharding import PartitionSpec as P

ITERS = 2
VEC = 128
TILE = 256
SLOTS = 24
N_ROW = 32
N_COL = 8
SIDE = 4
HALF = VEC // 2
PART = VEC // N_COL
NODES = N_ROW * N_COL * TILE
MESH = pl.DeviceIdType.MESH
F32 = jnp.float32
BF16 = jnp.bfloat16
PANEL = 8

T_FAR, T_NEAR, T_PREV_FAR, T_PREV_NEAR, T_LAST_FAR, T_LAST_NEAR = 0, 24, 48, 72, 96, 128
T_SIZE = 136
MAX_COPIES = 170


def split(value):
    high = value.astype(BF16)
    return high, (value - high.astype(F32)).astype(BF16)


def exact(a, b, dims):
    return lax.dot_general(
        a, b, (dims, ((), ())), precision=lax.Precision.HIGHEST, preferred_element_type=F32
    )


def three_pass(x, high, low, contract):
    dims = (((1,), (contract,)), ((), ()))
    xh, xl = split(x)
    both = lax.dot_general(
        jnp.concatenate([xh, xl], axis=0), high, dims, preferred_element_type=F32
    )
    rest = lax.dot_general(xh, low, dims, preferred_element_type=F32)
    return both[:VEC] + (both[VEC:] + rest)


def comm_scratch():
    block = lambda *lead: pltpu.VMEM((*lead, VEC, TILE), F32)
    half = lambda *lead: pltpu.VMEM((*lead, HALF, TILE), F32)
    return dict(
        far=block(N_ROW),
        near=block(N_COL),
        pack=block(16),
        sib=block(16),
        total=block(16),
        ring2a=half(2, 4),
        ring2b=block(2, 4),
        col=block(4),
        ring1a=half(2),
        ring1b=block(2),
        nears=block(N_COL),
        zin=block(2, 4),
        gram=pltpu.VMEM((VEC, VEC), F32),
        gz=pltpu.VMEM((N_COL, PART, VEC), F32),
        gx=pltpu.VMEM((N_COL, PART, VEC), F32),
        gy=pltpu.VMEM((SIDE, PART, VEC), F32),
        gsum=pltpu.VMEM((VEC, VEC), F32),
    )


def own_scratch():
    return dict(
        tiles_in=pltpu.VMEM((SLOTS, TILE, TILE), F32),
        high=pltpu.VMEM((SLOTS, TILE, TILE), BF16),
        low=pltpu.VMEM((SLOTS, TILE, TILE), BF16),
        sum_far=pltpu.VMEM((SLOTS + 1, VEC, TILE), F32),
        sum_near=pltpu.VMEM((SLOTS + 1, VEC, TILE), F32),
        upper=pltpu.VMEM((VEC, VEC), F32),
        inverse=pltpu.VMEM((VEC, VEC), F32),
        tile_sem=pltpu.SemaphoreType.DMA,
        send=pltpu.SemaphoreType.DMA((ITERS, MAX_COPIES)),
        recv=pltpu.SemaphoreType.DMA((ITERS, MAX_COPIES)),
    )


class Net:
    def __init__(self, send, recv):
        self.send, self.recv, self.copies = send, recv, []

    def copy(self, src, dst, device):
        i = len(self.copies)
        one = pltpu.make_async_remote_copy(
            src_ref=src,
            dst_ref=dst,
            send_sem=self.send.at[i],
            recv_sem=self.recv.at[i],
            device_id=device,
            device_id_type=MESH,
        )
        one.start()
        self.copies.append(one)
        return one

    def drain(self):
        for one in self.copies:
            one.wait_send()


def place():
    r = lax.axis_index("row")
    z = lax.axis_index("col")
    s = r % 2
    x = (r // 2) % SIDE
    y = r // (2 * SIDE)
    p1 = x * (1 - s) + y * s
    p2 = y * (1 - s) + x * s
    step1 = 2 + 6 * s
    step2 = 8 - 6 * s

    def dev(q1, q2):
        return ((q1 % SIDE) * step1 + (q2 % SIDE) * step2 + s, z)

    def slot(q1, q2):
        return s * 16 + (q2 % SIDE) * SIDE + q1 % SIDE

    return SimpleNamespace(
        r=r, z=z, s=s, x=x, y=y, p1=p1, p2=p2, slot=slot,
        r1p=dev(p1 + 1, p2), r1m=dev(p1 + 3, p2),
        r2p=dev(p1, p2 + 1), r2m=dev(p1, p2 + 3),
        sib=(r + 1 - 2 * s, z),
        zp=(r, (z + 1) % N_COL), zm=(r, (z + N_COL - 1) % N_COL),
        z_peer=lambda d: (r, (z + d) % N_COL),
        x_peer=lambda dx, ds: (y * 8 + ((x + dx) % SIDE) * 2 + (s + ds) % 2, z),
        y_peer=lambda dy: (((y + dy) % SIDE) * 8 + x * 2 + s, z),
    )


X_OFFSETS = [(dx, ds) for dx in range(SIDE) for ds in range(2) if dx or ds]
LOW, HIGH = pl.ds(0, HALF), pl.ds(HALF, HALF)
HALVES = (LOW, HIGH)


def enter(me):
    barrier = pltpu.get_barrier_semaphore()
    peers = [me.z_peer(d) for d in range(1, N_COL)]
    peers += [me.x_peer(*o) for o in X_OFFSETS]
    peers += [me.y_peer(d) for d in range(1, SIDE)]
    for peer in peers:
        pl.semaphore_signal(barrier, inc=1, device_id=peer, device_id_type=MESH)
    pl.semaphore_wait(barrier, len(peers))


def gather(me, net, buf, event):
    far, near = buf.far, buf.near
    p1, p2, z, slot = me.p1, me.p2, me.z, me.slot
    sib = []

    def send(block, rows, device):
        ref = far.at[block] if rows is None else far.at[block, rows]
        return net.copy(ref, ref, device)

    def share(block):
        sib.append(send(block, None, me.sib))

    def z_send(block, half, device):
        ref = near.at[block % N_COL, HALVES[half]]
        return net.copy(ref, ref, device)

    own = slot(p1, p2)
    r1 = [send(own, None, me.r1p), send(own, None, me.r1m)]
    zs = {}
    for h in range(2):
        zs["p", 1, h] = z_send(z, h, me.zp)
        zs["m", 1, h] = z_send(z, h, me.zm)
    r2 = [(send(own, None, me.r2p), send(own, None, me.r2m))]
    share(own)
    event("start")

    def z_step(d, h):
        if not (d == 4 and h == 1):
            zs["p", d, h].wait_recv()
            if d < 3 or (d == 3 and h == 0):
                zs["p", d + 1, h] = z_send(z + N_COL - d, h, me.zp)
        if not (d == 4 and h == 0):
            zs["m", d, h].wait_recv()
            if d < 3 or (d == 3 and h == 1):
                zs["m", d + 1, h] = z_send(z + d, h, me.zm)

    def column(block):
        r2.append((send(block, None, me.r2p), send(block, None, me.r2m)))
        share(block)

    across = []

    def ring2(i, q1):
        up, down = r2[i]
        up.wait_recv()
        first = send(slot(q1, p2 + 3), LOW, me.r2p)
        share(slot(q1, p2 + 3))
        down.wait_recv()
        second = send(slot(q1, p2 + 1), HIGH, me.r2m)
        share(slot(q1, p2 + 1))
        across.append((first, second, slot(q1, p2 + 2)))

    z_step(1, 0)
    r1[0].wait_recv()
    left = slot(p1 + 3, p2)
    r1a = send(left, LOW, me.r1p)
    column(left)
    r1[1].wait_recv()
    right = slot(p1 + 1, p2)
    r1b = send(right, HIGH, me.r1m)
    column(right)
    z_step(1, 1)
    event("gather")
    ring2(0, p1)
    event("gather")
    r1a.wait_recv()
    r1b.wait_recv()
    column(slot(p1 + 2, p2))
    z_step(2, 0)
    event("gather")
    z_step(2, 1)
    ring2(1, p1 + 3)
    event("gather")
    z_step(3, 0)
    ring2(2, p1 + 1)
    event("gather")
    z_step(3, 1)
    ring2(3, p1 + 2)
    event("gather")
    for first, second, block in across:
        first.wait_recv()
        second.wait_recv()
        share(block)
        event("gather")
    z_step(4, 0)
    z_step(4, 1)
    event("gather")
    for one in sib:
        one.wait_recv()


def mirror_products(tab, own, buf):
    @pl.loop(0, SLOTS)
    def _(k):
        x = buf.near[tab[T_NEAR + k]]
        res = three_pass(x, own.high[k], own.low[k], 0)
        own.sum_far[k + 1] = res + own.sum_far[tab[T_PREV_FAR + k]]


def upper_products(tab, own, buf):
    @pl.loop(0, SLOTS)
    def _(k):
        x = buf.far[tab[T_FAR + k]]
        res = three_pass(x, own.high[k], own.low[k], 1)
        own.sum_near[k + 1] = res + own.sum_near[tab[T_PREV_NEAR + k]]


def reduce(me, net, tab, own, buf, event):
    p1, p2, z, s = me.p1, me.p2, me.z, me.s
    total, pack = buf.total, buf.pack

    mirror_products(tab, own, buf)
    sib = []
    for q2 in (p1 + 2, p1 + 1, p1 + 3, p1):
        base = (q2 % SIDE) * SIDE
        for q1 in range(SIDE):
            pack[base + q1] = own.sum_far[tab[T_LAST_FAR + (1 - s) * 16 + base + q1]]
        sib.append(
            net.copy(pack.at[pl.ds(base, SIDE)], buf.sib.at[pl.ds(base, SIDE)], me.sib)
        )
    upper_products(tab, own, buf)

    nears = buf.nears
    for a in range(N_COL):
        nears[a] = own.sum_near[tab[T_LAST_NEAR + a]]
    zs = {}

    def z_send(sign, d, h):
        block = (z + d) % N_COL if sign == "p" else (z + N_COL - d) % N_COL
        zs[sign, d, h] = net.copy(
            nears.at[block, HALVES[h]],
            buf.zin.at[0 if sign == "p" else 1, d - 1, HALVES[h]],
            me.zp if sign == "p" else me.zm,
        )

    def z_add(sign, d, h):
        zs[sign, d + 1, h].wait_recv()
        block = (z + d) % N_COL if sign == "p" else (z + N_COL - d) % N_COL
        nears[block, HALVES[h]] += buf.zin[0 if sign == "p" else 1, d, HALVES[h]]

    z_send("p", 4, 0)
    z_send("m", 4, 1)
    z_send("p", 3, 1)
    z_send("m", 3, 0)

    order1 = (p1 + 2, p1 + 1, p1 + 3, p1)

    def at(q1, q2):
        return (q2 % SIDE) * SIDE + q1 % SIDE

    def whole(i, q2):
        sib[i].wait_recv()
        for q1 in range(SIDE):
            b = at(q1, q2)
            total[b] = own.sum_far[tab[T_LAST_FAR + s * 16 + b]] + buf.sib[b]

    whole(0, p2 + 2)
    a_copies = []
    for i, q1 in enumerate(order1):
        b = at(q1, p2 + 2)
        a_copies.append(
            (
                net.copy(total.at[b, LOW], buf.ring2a.at[0, i], me.r2p),
                net.copy(total.at[b, HIGH], buf.ring2a.at[1, i], me.r2m),
            )
        )
    event("reduce")
    z_add("p", 3, 0)
    z_send("p", 3, 0)
    z_add("m", 3, 1)
    z_send("m", 3, 1)
    whole(1, p2 + 1)
    whole(2, p2 + 3)
    b_copies = []
    for i, q1 in enumerate(order1):
        a_copies[i][0].wait_recv()
        b = at(q1, p2 + 1)
        total[b, LOW] += buf.ring2a[0, i]
        up = net.copy(total.at[b], buf.ring2b.at[0, i], me.r2p)
        a_copies[i][1].wait_recv()
        b = at(q1, p2 + 3)
        total[b, HIGH] += buf.ring2a[1, i]
        down = net.copy(total.at[b], buf.ring2b.at[1, i], me.r2m)
        b_copies.append((up, down))
        if i == 1:
            z_add("p", 2, 1)
            z_send("p", 2, 1)
            z_add("m", 2, 0)
            z_send("m", 2, 0)
            event("reduce")
    z_add("p", 2, 0)
    z_send("p", 2, 0)
    z_add("m", 2, 1)
    z_send("m", 2, 1)
    whole(3, p2)
    event("reduce")

    col = buf.col

    def gathered(i, q1):
        for one in b_copies[i]:
            one.wait_recv()
        col[i] = total[at(q1, p2)] + (buf.ring2b[0, i] + buf.ring2b[1, i])

    gathered(0, order1[0])
    a1 = net.copy(col.at[0, LOW], buf.ring1a.at[0], me.r1p)
    a2 = net.copy(col.at[0, HIGH], buf.ring1a.at[1], me.r1m)
    z_add("p", 1, 1)
    z_send("p", 1, 1)
    z_add("m", 1, 0)
    z_send("m", 1, 0)
    event("reduce")
    gathered(1, order1[1])
    a1.wait_recv()
    col[1, LOW] += buf.ring1a[0]
    b1 = net.copy(col.at[1], buf.ring1b.at[0], me.r1p)
    event("reduce")
    gathered(2, order1[2])
    a2.wait_recv()
    col[2, HIGH] += buf.ring1a[1]
    b2 = net.copy(col.at[2], buf.ring1b.at[1], me.r1m)
    z_add("p", 1, 0)
    z_send("p", 1, 0)
    z_add("m", 1, 1)
    z_send("m", 1, 1)
    event("reduce")
    gathered(3, order1[3])
    for sign in "pm":
        for h in range(2):
            z_add(sign, 0, h)
            if sign == "p" and h == 1:
                event("reduce")
    b1.wait_recv()
    b2.wait_recv()
    return (col[3] + nears[z]) + (buf.ring1b[0] + buf.ring1b[1])


def gram_steps(me, net, own, buf, image):
    buf.gram[...] = exact(image, image, ((1,), (1,))) * (1.0 / NODES)
    gz, gx, gy, gsum = buf.gz, buf.gx, buf.gy, buf.gsum

    def rows(c):
        return pl.ds(pl.multiple_of((c % N_COL) * PART, PART), PART)

    ones = [
        net.copy(buf.gram.at[rows(me.z + d)], gz.at[d], me.z_peer(d)) for d in range(1, N_COL)
    ]
    yield
    for one in ones:
        one.wait_recv()
    part = buf.gram[rows(me.z), :]
    for d in range(1, N_COL):
        part = part + gz[d]
    here = me.x * 2 + me.s
    gx[here] = part
    ones = [net.copy(gx.at[here], gx.at[here], me.x_peer(*o)) for o in X_OFFSETS]
    yield
    for one in ones:
        one.wait_recv()
    part = gx[0]
    for i in range(1, N_COL):
        part = part + gx[i]
    gy[me.y] = part
    ones = [net.copy(gy.at[me.y], gy.at[me.y], me.y_peer(d)) for d in range(1, SIDE)]
    yield
    for one in ones:
        one.wait_recv()
    part = gy[0]
    for i in range(1, SIDE):
        part = part + gy[i]
    gsum[rows(me.z), :] = part
    ones = [
        net.copy(gsum.at[rows(me.z)], gsum.at[rows(me.z)], me.z_peer(d))
        for d in range(1, N_COL)
    ]
    yield
    for one in ones:
        one.wait_recv()
    yield from cholesky_steps(own, gsum)


def cholesky_steps(own, gsum):
    upper, inverse = own.upper, own.inverse
    lane = lax.broadcasted_iota(jnp.int32, (VEC, VEC), 1)
    sub = lax.broadcasted_iota(jnp.int32, (VEC, VEC), 0)
    upper[...] = gsum[...]
    inverse[...] = jnp.where(lane == sub, 1.0, 0.0).astype(F32)
    for panel in range(0, VEC, PANEL):
        @pl.loop(panel, panel + PANEL)
        def _(j):
            row = upper[pl.ds(j, 1), :]
            row_inv = inverse[pl.ds(j, 1), :]
            pivot = jnp.sum(jnp.where(lane[:1] == j, row, 0.0), axis=1, keepdims=True)
            scale = 1.0 / jnp.sqrt(pivot)
            m = upper[...]
            below = (lane == j) & (sub > j)
            column = jnp.sum(jnp.where(below, m, 0.0), axis=1, keepdims=True) * scale
            u = row * scale
            v = row_inv * scale
            here = sub == j
            upper[...] = jnp.where(here, u, m - column * u)
            inverse[...] = jnp.where(here, v, inverse[...] - column * v)
        yield


def kernel(names, tab, start, tiles, basis, factor, *scratch):
    own_names, comm_names = names
    own = SimpleNamespace(**dict(zip(own_names, scratch)))
    rest = scratch[len(own_names):]
    bufs = [
        SimpleNamespace(**dict(zip(comm_names, rest[it * len(comm_names):])))
        for it in range(ITERS)
    ]
    me = place()
    loading = pltpu.make_async_copy(tiles, own.tiles_in, own.tile_sem)
    loading.start()
    image = start[...].T
    own.sum_far[0] = jnp.zeros((VEC, TILE), F32)
    own.sum_near[0] = jnp.zeros((VEC, TILE), F32)
    enter(me)

    for it in range(ITERS):
        buf = bufs[it]
        net = Net(own.send.at[it], own.recv.at[it])
        if it:
            steps = gram_steps(me, net, own, bufs[it - 1], image)
        buf.far[me.slot(me.p1, me.p2)] = image
        buf.near[me.z] = image

        def event(where):
            if it:
                next(steps, None)
            elif where == "start":
                loading.wait()

                @pl.loop(0, SLOTS)
                def _(k):
                    own.high[k], own.low[k] = split(own.tiles_in[k])

        gather(me, net, buf, event)
        image = reduce(me, net, tab, own, buf, event)
        if it:
            for _ in steps:
                pass
            image = exact(own.inverse[...], image, ((1,), (0,)))
            for _ in gram_steps(me, net, own, buf, image):
                pass
        net.drain()
    basis[...] = exact(own.inverse[...], image, ((1,), (0,))).T
    lane = lax.broadcasted_iota(jnp.int32, (VEC, VEC), 1)
    sub = lax.broadcasted_iota(jnp.int32, (VEC, VEC), 0)
    factor[...] = jnp.where(lane >= sub, own.upper[...], 0.0).T


def far_slot(b):
    s, x, y = b % 2, (b // 2) % SIDE, b // (2 * SIDE)
    return jnp.where(s == 0, y * SIDE + x, 16 + x * SIDE + y)


def table(rows, cols, count):
    slot = jnp.arange(SLOTS, dtype=jnp.int32)
    far = far_slot(cols)

    def latest(keys, blocks):
        asked = jnp.concatenate([keys, jnp.arange(blocks, dtype=jnp.int32)])
        before = jnp.concatenate([slot, jnp.full((blocks,), SLOTS, jnp.int32)])
        hit = (asked[:, None] == keys[None, :]) & (slot[None, :] < before[:, None])
        hit = hit & (slot[None, :] < count)
        return jnp.max(jnp.where(hit, slot[None, :] + 1, 0), axis=1)

    by_far = latest(far, N_ROW)
    by_near = latest(rows, N_COL)
    return jnp.concatenate(
        [far, rows, by_far[:SLOTS], by_near[:SLOTS], by_far[SLOTS:], by_near[SLOTS:]]
    )


def shards(start, tiles, tile_rows, tile_cols, tile_count):
    own, comm = own_scratch(), comm_scratch()
    names = (tuple(own), tuple(comm))
    vmem = pl.BlockSpec(memory_space=pltpu.VMEM)

    def body(*refs):
        kernel(names, *refs)

    return pl.pallas_call(
        body,
        out_shape=(
            jax.ShapeDtypeStruct((TILE, VEC), F32),
            jax.ShapeDtypeStruct((VEC, VEC), F32),
        ),
        in_specs=[
            pl.BlockSpec(memory_space=pltpu.SMEM),
            vmem,
            pl.BlockSpec(memory_space=pl.ANY),
        ],
        out_specs=(vmem, vmem),
        scratch_shapes=[*own.values(), *(ref for _ in range(ITERS) for ref in comm.values())],
        compiler_params=pltpu.CompilerParams(
            collective_id=0, has_side_effects=True, vmem_limit_bytes=62 * 1024 * 1024
        ),
    )(table(tile_rows[0], tile_cols[0], tile_count[0]), start, tiles[0])


def solution(mesh):
    placed = (
        P(("row", "col"), None),
        P(("row", "col"), None, None, None),
        P(("row", "col"), None),
        P(("row", "col"), None),
        P(("row", "col")),
    )
    return jax.shard_map(
        shards,
        mesh=mesh,
        in_specs=placed,
        out_specs=(P(("row", "col"), None), P()),
        check_vma=False,
    )
```

time: 1020 us -> 167 us (0.16)
  waiting for transfers between devices: 842 us -> 0 us
  Pallas kernels: 0 us -> 157 us
  matrix products: 60.7 us -> 0 us
  other arithmetic: 50.4 us -> 3.68 us
  local copies, waits for them, and re-layouts: 40.6 us -> 4.49 us
  between operations: 15.2 us -> 1.31 us
    psum x2 -> x0, waiting for transfers between devices: 492 us -> none  [shards(): gram = lax.psum(local_gram, ('row', 'col')) / total_nodes]
    reduce_scatter x4 -> x0, waiting for transfers between devices: 212 us -> none  [the longest x2 138 us: shards(): lax.psum_scatter(far_part, 'row', scatter_dimension=0, tiled=True)]
    pallas_call x0 -> x1, Pallas kernels: none -> 157 us  [shards(): pl.pallas_call(body, out_shape=(jax.ShapeDtypeStruct((TILE, VEC), F32), j...]
    all_gather x4 -> x0, waiting for transfers between devices: 136 us -> none  [the longest x2 70.3 us: spread(): far = lax.all_gather(vectors, 'row', axis=0, tiled=True)]
    dot_general x10 -> x0, matrix products: 57.5 us -> none  [the longest x2 22.2 us: products(): jnp.einsum('kpq,kqf->kpf', pieces, far_blocks[cols], precision=lax.Precis...]
    another operation x10 -> x0, other arithmetic: 46.3 us -> none  [the longest x6 24.8 us: shards(): factor = jnp.linalg.cholesky(gram)]
    dot_general x8 -> x0, local copies, waits for them, and re-layouts: 22.1 us -> none  [the longest x2 8.77 us: products(): jnp.einsum('kb,kpf->bpf', pick_far, mirror, precision=lax.Precision.HIGHEST)]
    gather x4 -> x0, local copies, waits for them, and re-layouts: 10.3 us -> none  [the longest x2 5.87 us: products(): far_blocks[cols]]
  transfers between devices with their start and end apart: 10 -> 0, of which waited for: 10 -> 0; matrix products, arithmetic and copies ran while one was open for 9% -> 0% of each run, Pallas kernels for 0% -> 0%
where the time goes in v1:
time: 167 us; the launch traced here: 166 us
  Pallas kernels  157 us (94%)
  local copies, waits for them, and re-layouts  4.49 us (3%)
  other arithmetic  3.68 us (2%)
    pallas_call x1, Pallas kernels, shards(): pl.pallas_call(body, out_shape=(jax.ShapeDtypeStruct((TILE, VEC), F32), j...  157 us

profile of v1, /device:TPU:1, one launch (start us, length us, event | category | flops | bytes accessed | tf_op | source)
XLA Modules:
  0.0 166.5 jit_solution(2158972997552123470)
XLA Ops:
  1.3 0.7 compare_select_fusion.5
  2.0 0.7 fusion.6
  2.7 0.7 pad_add_fusion.1
  3.4 0.8 select_reduce_fusion
  4.2 0.1 slice.15
  4.2 0.1 pad_add_fusion
  4.3 0.7 select_reduce_fusion.1
  5.1 0.1 slice.14
  5.1 1.3 concatenate.13.refs_0_
  6.4 157.0 %shard_map.68 = (f32[256,128]{1,0:T(8,128)}, f32[128,128]{1,0:T(8,128)}) custom-call(s32[136]{0:T(256)} %concatenate.13.refs_0_, f32[256,128]{1,0:T(8,128)} %refs_1_.1, f32[24,256,256]{2,1,0:T(8,128)} %bitcast.24), custom_call_target="tpu_custom_call" | custom-call | tf_op jit(solution)/shard_map/pallas_call | solution.py:542
  163.5 1.6 copy.10
  165.0 1.5 copy.11
  (4 shorter events, 0.0 us)

commit v2 on v1

v2 whole, which is shorter than its diff:
```python
from types import SimpleNamespace

import jax
import jax.numpy as jnp
from jax import lax
from jax.experimental import pallas as pl
from jax.experimental.pallas import tpu as pltpu
from jax.sharding import PartitionSpec as P

ITERS = 2
VEC = 128
TILE = 256
SLOTS = 24
N_ROW = 32
N_COL = 8
SIDE = 4
HALF = VEC // 2
PART = VEC // N_COL
NODES = N_ROW * N_COL * TILE
MESH = pl.DeviceIdType.MESH
F32 = jnp.float32
BF16 = jnp.bfloat16
PANEL = 32
GROUP = 16
UNROLL = 8
LAG = 0

T_PREV_FAR, T_PREV_NEAR, T_LAST_FAR, T_LAST_NEAR, T_FAR = 0, 24, 48, 80, 88
T_SIZE = 112
MAX_COPIES = 320


def split(value):
    high = value.astype(BF16)
    return high, (value - high.astype(F32)).astype(BF16)


def exact(a, b, dims):
    return lax.dot_general(
        a, b, (dims, ((), ())), precision=lax.Precision.HIGHEST, preferred_element_type=F32
    )


def three_pass(x, high, low, contract):
    dims = (((1,), (contract,)), ((), ()))
    xh, xl = split(x)
    both = lax.dot_general(
        jnp.concatenate([xh, xl], axis=0), high, dims, preferred_element_type=F32
    )
    rest = lax.dot_general(xh, low, dims, preferred_element_type=F32)
    return both[: x.shape[0]] + (both[x.shape[0] :] + rest)


def half_scratch():
    block = lambda *lead: pltpu.VMEM((*lead, HALF, TILE), F32)
    return dict(
        far=block(N_ROW),
        near=block(N_COL),
        pack=block(16),
        sib=block(16),
        total=block(16),
        ring2a=block(4),
        ring2b=block(2, 4),
        col=block(4),
        ring1a=block(1),
        ring1b=block(2),
        nears=block(N_COL),
        zin=block(2, 4),
    )


def gram_scratch():
    return dict(
        image=pltpu.VMEM((VEC, TILE), F32),
        gram=pltpu.VMEM((VEC, VEC), F32),
        gz=pltpu.VMEM((N_COL, PART, VEC), F32),
        gx=pltpu.VMEM((N_COL, PART, VEC), F32),
        gy=pltpu.VMEM((SIDE, PART, VEC), F32),
        gsum=pltpu.VMEM((VEC, VEC), F32),
    )


def own_scratch():
    sums = lambda: pltpu.VMEM((SLOTS + 1, HALF, TILE), F32)
    return dict(
        table=pltpu.SMEM((T_SIZE,), jnp.int32),
        tiles_in=pltpu.VMEM((SLOTS, TILE, TILE), F32),
        high=pltpu.VMEM((SLOTS, TILE, TILE), BF16),
        low=pltpu.VMEM((SLOTS, TILE, TILE), BF16),
        sum_far0=sums(),
        sum_far1=sums(),
        sum_near0=sums(),
        sum_near1=sums(),
        upper=pltpu.VMEM((VEC, VEC), F32),
        inverse=pltpu.VMEM((VEC, VEC), F32),
        tile_sem=pltpu.SemaphoreType.DMA,
        send=pltpu.SemaphoreType.DMA((MAX_COPIES,)),
        recv=pltpu.SemaphoreType.DMA((MAX_COPIES,)),
    )


class Net:
    def __init__(self, send, recv):
        self.send, self.recv, self.copies = send, recv, []

    def copy(self, src, dst, device):
        i = len(self.copies)
        one = pltpu.make_async_remote_copy(
            src_ref=src,
            dst_ref=dst,
            send_sem=self.send.at[i],
            recv_sem=self.recv.at[i],
            device_id=device,
            device_id_type=MESH,
        )
        one.start()
        self.copies.append(one)
        return one

    def drain(self):
        for one in self.copies:
            one.wait_send()


def place():
    r = lax.axis_index("row")
    z = lax.axis_index("col")
    s = r % 2
    x = (r // 2) % SIDE
    y = r // (2 * SIDE)
    p1 = x * (1 - s) + y * s
    p2 = y * (1 - s) + x * s
    step1 = 2 + 6 * s
    step2 = 8 - 6 * s

    def dev(q1, q2):
        return ((q1 % SIDE) * step1 + (q2 % SIDE) * step2 + s, z)

    def slot(q1, q2):
        return s * 16 + (q2 % SIDE) * SIDE + q1 % SIDE

    return SimpleNamespace(
        r=r, z=z, s=s, x=x, y=y, p1=p1, p2=p2, slot=slot,
        r1p=dev(p1 + 1, p2), r1m=dev(p1 + 3, p2),
        r2p=dev(p1, p2 + 1), r2m=dev(p1, p2 + 3),
        sib=(r + 1 - 2 * s, z),
        zp=(r, (z + 1) % N_COL), zm=(r, (z + N_COL - 1) % N_COL),
        z_peer=lambda d: (r, (z + d) % N_COL),
        x_peer=lambda dx, ds: (y * 8 + ((x + dx) % SIDE) * 2 + (s + ds) % 2, z),
        y_peer=lambda dy: (((y + dy) % SIDE) * 8 + x * 2 + s, z),
    )


X_OFFSETS = [(dx, ds) for dx in range(SIDE) for ds in range(2) if dx or ds]


def enter(me):
    barrier = pltpu.get_barrier_semaphore()
    peers = [me.z_peer(d) for d in range(1, N_COL)]
    peers += [me.x_peer(*o) for o in X_OFFSETS]
    peers += [me.y_peer(d) for d in range(1, SIDE)]
    for peer in peers:
        pl.semaphore_signal(barrier, inc=1, device_id=peer, device_id_type=MESH)
    pl.semaphore_wait(barrier, len(peers))


def gather_steps(h, me, net, buf):
    far, near = buf.far, buf.near
    p1, p2, z, slot = me.p1, me.p2, me.z, me.slot
    sib, r2, across = [], [], []
    zs = {}

    def send(block, device):
        return net.copy(far.at[block], far.at[block], device)

    def share(block):
        sib.append(send(block, me.sib))

    def z_send(block, device):
        ref = near.at[block % N_COL]
        return net.copy(ref, ref, device)

    def z_step(d):
        if d < 4 or h == 0:
            zs["p", d].wait_recv()
            if d < 3 or (d == 3 and h == 0):
                zs["p", d + 1] = z_send(z + N_COL - d, me.zp)
        if d < 4 or h == 1:
            zs["m", d].wait_recv()
            if d < 3 or (d == 3 and h == 1):
                zs["m", d + 1] = z_send(z + d, me.zm)

    def column(block):
        r2.append((send(block, me.r2p), send(block, me.r2m)))
        share(block)

    def ring2(i, q1):
        up, down = r2[i]
        up.wait_recv()
        if h == 0:
            on = send(slot(q1, p2 + 3), me.r2p)
        share(slot(q1, p2 + 3))
        down.wait_recv()
        if h == 1:
            on = send(slot(q1, p2 + 1), me.r2m)
        share(slot(q1, p2 + 1))
        across.append((on, slot(q1, p2 + 2)))

    own = slot(p1, p2)
    r1 = [send(own, me.r1p), send(own, me.r1m)]
    zs["p", 1] = z_send(z, me.zp)
    zs["m", 1] = z_send(z, me.zm)
    column(own)
    yield
    r1[0].wait_recv()
    if h == 0:
        on = send(slot(p1 + 3, p2), me.r1p)
    column(slot(p1 + 3, p2))
    r1[1].wait_recv()
    if h == 1:
        on = send(slot(p1 + 1, p2), me.r1m)
    column(slot(p1 + 1, p2))
    yield
    z_step(1)
    yield
    ring2(0, p1)
    yield
    on.wait_recv()
    column(slot(p1 + 2, p2))
    yield
    z_step(2)
    yield
    ring2(1, p1 + 3)
    yield
    ring2(2, p1 + 1)
    yield
    z_step(3)
    yield
    ring2(3, p1 + 2)
    yield
    for i, (one, block) in enumerate(across):
        one.wait_recv()
        share(block)
        if i % 2:
            yield
    z_step(4)
    yield
    for one in sib:
        one.wait_recv()


def mirror_products(rows, own, buf, sum_far):
    @pl.loop(0, SLOTS, unroll=UNROLL)
    def _(k):
        x = buf.near[rows[0, k]]
        res = three_pass(x, own.high[k], own.low[k], 0)
        sum_far[k + 1] = res + sum_far[own.table[T_PREV_FAR + k]]


def upper_products(own, buf, sum_near):
    @pl.loop(0, SLOTS, unroll=UNROLL)
    def _(k):
        x = buf.far[own.table[T_FAR + k]]
        res = three_pass(x, own.high[k], own.low[k], 1)
        sum_near[k + 1] = res + sum_near[own.table[T_PREV_NEAR + k]]


def reduce_steps(h, me, net, rows, own, buf, result):
    p1, p2, z, s = me.p1, me.p2, me.z, me.s
    total, pack, nears, tab = buf.total, buf.pack, buf.nears, own.table
    sum_far = (own.sum_far0, own.sum_far1)[h]
    sum_near = (own.sum_near0, own.sum_near1)[h]

    mirror_products(rows, own, buf, sum_far)
    sib = []
    for q2 in (p1 + 2, p1 + 1, p1 + 3, p1):
        base = (q2 % SIDE) * SIDE
        for q1 in range(SIDE):
            pack[base + q1] = sum_far[tab[T_LAST_FAR + (1 - s) * 16 + base + q1]]
        sib.append(
            net.copy(pack.at[pl.ds(base, SIDE)], buf.sib.at[pl.ds(base, SIDE)], me.sib)
        )
    yield
    upper_products(own, buf, sum_near)
    for a in range(N_COL):
        nears[a] = sum_near[tab[T_LAST_NEAR + a]]
    zs = {}
    order1 = (p1 + 2, p1 + 1, p1 + 3, p1)

    def z_block(sign, d):
        return (z + d) % N_COL if sign == "p" else (z + N_COL - d) % N_COL

    def z_send(sign, d):
        zs[sign, d] = net.copy(
            nears.at[z_block(sign, d)],
            buf.zin.at[0 if sign == "p" else 1, d - 1],
            me.zp if sign == "p" else me.zm,
        )

    def z_add(sign, d):
        if (sign, d + 1) in zs:
            zs[sign, d + 1].wait_recv()
            nears[z_block(sign, d)] += buf.zin[0 if sign == "p" else 1, d]

    def z_step(d):
        for sign in "pm":
            z_add(sign, d)
            z_send(sign, d)

    def at(q1, q2):
        return (q2 % SIDE) * SIDE + q1 % SIDE

    def whole(i, q2):
        sib[i].wait_recv()
        for q1 in range(SIDE):
            b = at(q1, q2)
            total[b] = sum_far[tab[T_LAST_FAR + s * 16 + b]] + buf.sib[b]

    z_send("pm"[h], 4)
    z_send("mp"[h], 3)
    whole(0, p2 + 2)
    ahead = [
        net.copy(total.at[at(q1, p2 + 2)], buf.ring2a.at[i], (me.r2p, me.r2m)[h])
        for i, q1 in enumerate(order1)
    ]
    plain, summed = ((p2 + 3, p2 + 1), (p2 + 1, p2 + 3))[h]
    whole((2, 1)[h], plain)
    plain_copies = [
        net.copy(total.at[at(q1, plain)], buf.ring2b.at[1 - h, i], (me.r2m, me.r2p)[h])
        for i, q1 in enumerate(order1)
    ]
    whole((1, 2)[h], summed)
    yield
    sign = "pm"[h]
    z_add(sign, 3)
    z_send(sign, 3)
    yield
    summed_copies = []
    for i, q1 in enumerate(order1):
        ahead[i].wait_recv()
        b = at(q1, summed)
        total[b] += buf.ring2a[i]
        summed_copies.append(net.copy(total.at[b], buf.ring2b.at[h, i], (me.r2p, me.r2m)[h]))
        if i == 1:
            yield
    whole(3, p2)
    yield
    z_step(2)
    yield
    col = buf.col

    def gathered(i):
        plain_copies[i].wait_recv()
        summed_copies[i].wait_recv()
        col[i] = total[at(order1[i], p2)] + (buf.ring2b[0, i] + buf.ring2b[1, i])

    gathered(0)
    on = net.copy(col.at[0], buf.ring1a.at[0], (me.r1p, me.r1m)[h])
    yield
    gathered(2 - h)
    b1 = net.copy(col.at[2 - h], buf.ring1b.at[1 - h], (me.r1m, me.r1p)[h])
    yield
    z_step(1)
    yield
    gathered(1 + h)
    on.wait_recv()
    col[1 + h] += buf.ring1a[0]
    b2 = net.copy(col.at[1 + h], buf.ring1b.at[h], (me.r1p, me.r1m)[h])
    gathered(3)
    yield
    z_add("p", 0)
    z_add("m", 0)
    part = col[3] + nears[z]
    yield
    b1.wait_recv()
    b2.wait_recv()
    part = part + (buf.ring1b[0] + buf.ring1b[1])
    result[HALF * h : HALF * (h + 1), :] = part


def pipe_steps(h, me, net, rows, own, bufs, grams, first):
    for it in range(ITERS):
        buf = bufs[it][h]
        image = first if it == 0 else grams[it - 1].image[HALF * h : HALF * (h + 1), :]
        buf.far[me.slot(me.p1, me.p2)] = image
        buf.near[me.z] = image
        yield from gather_steps(h, me, net, buf)
        yield
        yield from reduce_steps(h, me, net, rows, own, buf, grams[it].image)
        yield ("done", it)


def gram_steps(me, net, own, buf, image):
    buf.gram[...] = exact(image, image, ((1,), (1,))) * (1.0 / NODES)
    gz, gx, gy, gsum = buf.gz, buf.gx, buf.gy, buf.gsum

    def rows(c):
        return pl.ds(pl.multiple_of((c % N_COL) * PART, PART), PART)

    ones = [
        net.copy(buf.gram.at[rows(me.z + d)], gz.at[d], me.z_peer(d)) for d in range(1, N_COL)
    ]
    yield
    for one in ones:
        one.wait_recv()
    part = buf.gram[rows(me.z), :]
    for d in range(1, N_COL):
        part = part + gz[d]
    here = me.x * 2 + me.s
    gx[here] = part
    ones = [net.copy(gx.at[here], gx.at[here], me.x_peer(*o)) for o in X_OFFSETS]
    yield
    for one in ones:
        one.wait_recv()
    part = gx[0]
    for i in range(1, N_COL):
        part = part + gx[i]
    gy[me.y] = part
    ones = [net.copy(gy.at[me.y], gy.at[me.y], me.y_peer(d)) for d in range(1, SIDE)]
    yield
    for one in ones:
        one.wait_recv()
    part = gy[0]
    for i in range(1, SIDE):
        part = part + gy[i]
    gsum[rows(me.z), :] = part
    ones = [
        net.copy(gsum.at[rows(me.z)], gsum.at[rows(me.z)], me.z_peer(d))
        for d in range(1, N_COL)
    ]
    yield
    for one in ones:
        one.wait_recv()
    yield
    yield from cholesky_steps(own, gsum)


def cholesky_steps(own, gsum):
    upper, inverse = own.upper, own.inverse
    lane = lax.broadcasted_iota(jnp.int32, (VEC, VEC), 1)
    sub = lax.broadcasted_iota(jnp.int32, (VEC, VEC), 0)
    upper[...] = gsum[...]
    inverse[...] = jnp.where(lane == sub, 1.0, 0.0).astype(F32)
    strip = sub[:PANEL]
    for o in range(0, VEC, PANEL):
        p = upper[o : o + PANEL, :]
        a = inverse[o : o + PANEL, :]
        for first in range(0, PANEL, GROUP):
            columns = [
                jnp.broadcast_to(p[:, o + j : o + j + 1], (PANEL, VEC))
                for j in range(first, first + GROUP)
            ]
            for t in range(GROUP):
                j = first + t
                if j == PANEL - 1:
                    continue
                c = columns[t]
                m = jnp.where(strip > j, c, 0.0) * (1.0 / c[j : j + 1])
                for w in range(t + 1, GROUP):
                    columns[w] = columns[w] - m * c[first + w : first + w + 1]
                p, a = p - m * p[j : j + 1], a - m * a[j : j + 1]
        pivots = jnp.sum(jnp.where(lane[:PANEL] == strip + o, p, 0.0), axis=1, keepdims=True)
        scale = 1.0 / jnp.sqrt(pivots)
        p, a = p * scale, a * scale
        upper[o : o + PANEL, :] = p
        inverse[o : o + PANEL, :] = a
        if o + PANEL < VEC:
            below = p.T[o + PANEL :]
            upper[o + PANEL :, :] -= exact(below, p, ((1,), (0,)))
            inverse[o + PANEL :, :] -= exact(below, a, ((1,), (0,)))
        yield


def prepare_steps(rows, cols, count, own, loading):
    tab = own.table
    live = count[0]

    def latest(keys, key, before):
        found = jnp.int32(0)
        for k in range(SLOTS):
            hit = (keys[k] == key) & (k < before)
            found = jnp.where(hit, k + 1, found)
        return found

    cols_at = [cols[0, k] for k in range(SLOTS)]
    rows_at = [rows[0, k] for k in range(SLOTS)]

    @pl.loop(0, SLOTS)
    def _(k):
        b = cols[0, k]
        s, x, y = b % 2, (b // 2) % SIDE, b // (2 * SIDE)
        tab[T_FAR + k] = s * 16 + jnp.where(s == 0, y * SIDE + x, x * SIDE + y)
        tab[T_PREV_FAR + k] = latest(cols_at, b, jnp.minimum(k, live))
        tab[T_PREV_NEAR + k] = latest(rows_at, rows[0, k], jnp.minimum(k, live))

    yield

    @pl.loop(0, N_ROW)
    def _(i):
        s, q2, q1 = i // 16, (i // SIDE) % SIDE, i % SIDE
        x, y = q1 * (1 - s) + q2 * s, q2 * (1 - s) + q1 * s
        tab[T_LAST_FAR + i] = latest(cols_at, y * 8 + x * 2 + s, live)

    @pl.loop(0, N_COL)
    def _(i):
        tab[T_LAST_NEAR + i] = latest(rows_at, i, live)

    yield
    loading.wait()
    for first in range(0, SLOTS, 6):

        @pl.loop(first, first + 6)
        def _(k):
            own.high[k], own.low[k] = split(own.tiles_in[k])

        yield


def kernel(names, rows, cols, count, start, tiles, basis, factor, *scratch):
    own_names, gram_names, half_names = names
    refs = iter(scratch)
    take = lambda keys: SimpleNamespace(**{key: next(refs) for key in keys})
    own = take(own_names)
    grams = [take(gram_names) for _ in range(ITERS)]
    bufs = [[take(half_names) for _ in range(2)] for _ in range(ITERS)]
    me = place()
    loading = pltpu.make_async_copy(tiles, own.tiles_in, own.tile_sem)
    loading.start()
    image = start[...].T
    for ref in (own.sum_far0, own.sum_far1, own.sum_near0, own.sum_near1):
        ref[0] = jnp.zeros((HALF, TILE), F32)
    enter(me)

    net = Net(own.send, own.recv)
    pipes = [
        pipe_steps(h, me, net, rows, own, bufs, grams, image[HALF * h : HALF * (h + 1)])
        for h in range(2)
    ]
    beside = prepare_steps(rows, cols, count, own, loading)
    done = [None, None]
    tick = 0
    while any(d != ("done", ITERS - 1) for d in done):
        for h in range(2):
            if h == 0 or tick >= LAG:
                at = next(pipes[h], None)
                if at is not None:
                    done[h] = at
                    if at == ("done", 0) and done[1 - h] == ("done", 0):
                        beside = gram_steps(me, net, own, grams[0], grams[0].image[...])
        next(beside, None)
        tick += 1
    for _ in beside:
        pass
    image = exact(own.inverse[...], grams[1].image[...], ((1,), (0,)))
    for _ in gram_steps(me, net, own, grams[1], image):
        pass
    basis[...] = exact(own.inverse[...], image, ((1,), (0,))).T
    lane = lax.broadcasted_iota(jnp.int32, (VEC, VEC), 1)
    sub = lax.broadcasted_iota(jnp.int32, (VEC, VEC), 0)
    factor[...] = jnp.where(lane >= sub, own.upper[...], 0.0).T
    net.drain()


def shards(start, tiles, tile_rows, tile_cols, tile_count):
    own, gram, half = own_scratch(), gram_scratch(), half_scratch()
    names = (tuple(own), tuple(gram), tuple(half))
    vmem = pl.BlockSpec(memory_space=pltpu.VMEM)
    smem = pl.BlockSpec(memory_space=pltpu.SMEM)

    def body(*refs):
        kernel(names, *refs)

    return pl.pallas_call(
        body,
        out_shape=(
            jax.ShapeDtypeStruct((TILE, VEC), F32),
            jax.ShapeDtypeStruct((VEC, VEC), F32),
        ),
        in_specs=[smem, smem, smem, vmem, pl.BlockSpec(memory_space=pl.ANY)],
        out_specs=(vmem, vmem),
        scratch_shapes=[
            *own.values(),
            *(ref for _ in range(ITERS) for ref in gram.values()),
            *(ref for _ in range(2 * ITERS) for ref in half.values()),
        ],
        compiler_params=pltpu.CompilerParams(
            collective_id=0, has_side_effects=True, vmem_limit_bytes=62 * 1024 * 1024
        ),
    )(tile_rows, tile_cols, tile_count, start, tiles[0])


def solution(mesh):
    placed = (
        P(("row", "col"), None),
        P(("row", "col"), None, None, None),
        P(("row", "col"), None),
        P(("row", "col"), None),
        P(("row", "col")),
    )
    return jax.shard_map(
        shards,
        mesh=mesh,
        in_specs=placed,
        out_specs=(P(("row", "col"), None), P()),
        check_vma=False,
    )
```

time: 167 us -> 137 us (0.82)
  Pallas kernels: 157 us -> 132 us
  other arithmetic: 3.68 us -> 0 us
    pallas_call x1, Pallas kernels: 157 us -> 132 us  [shards(): pl.pallas_call(body, out_shape=(jax.ShapeDtypeStruct((TILE, VEC), F32), j...]
where the time goes in v2:
time: 137 us; the launch traced here: 136 us
  Pallas kernels  132 us (96%)
  local copies, waits for them, and re-layouts  3.04 us (2%)
    pallas_call x1, Pallas kernels, shards(): pl.pallas_call(body, out_shape=(jax.ShapeDtypeStruct((TILE, VEC), F32), j...  132 us
    unnamed x2, local copies, waits for them, and re-layouts  3.04 us

profile of v2, /device:TPU:1, one launch (start us, length us, event | category | flops | bytes accessed | tf_op | source)
XLA Modules:
  0.0 136.4 jit_solution(11393671341421488735)
XLA Ops:
  1.3 132.1 %shard_map.68 = (f32[256,128]{1,0:T(8,128)}, f32[128,128]{1,0:T(8,128)}) custom-call(s32[1,24]{1,0:T(1,128)} %refs_0_.1, s32[1,24]{1,0:T(1,128)} %refs_1_.1, s32[1]{0:T(128)S(6)} %copy.9.refs_2_, f32[256,128]{1,0:T(8,128)} %refs_3_.1, f32[24,256,256]{2,1,0:T(8,128)} %bitcast.1), custom_call_target="tpu_custom_call" | custom-call | tf_op jit(solution)/shard_map/pallas_call | solution.py:573
  133.3 1.6 %copy.10 = f32[256,128]{1,0:T(8,128)} copy(f32[256,128]{1,0:T(8,128)} %get-tuple-element.4) | data formatting | bytes 262144
  134.9 1.5 %copy.11 = f32[128,128]{1,0:T(8,128)} copy(f32[128,128]{1,0:T(8,128)} %get-tuple-element.5) | data formatting | bytes 131072

commit v3 on v2

--- a/solution.py
+++ b/solution.py
@@ -14,7 +14,6 @@
 N_ROW = 32
 N_COL = 8
 SIDE = 4
-HALF = VEC // 2
 PART = VEC // N_COL
 NODES = N_ROW * N_COL * TILE
 MESH = pl.DeviceIdType.MESH
@@ -23,7 +22,8 @@
 PANEL = 32
 GROUP = 16
 UNROLL = 8
-LAG = 0
+EVERY = 3
+PIECES = 2
 
 T_PREV_FAR, T_PREV_NEAR, T_LAST_FAR, T_LAST_NEAR, T_FAR = 0, 24, 48, 80, 88
 T_SIZE = 112
@@ -51,8 +51,8 @@
     return both[: x.shape[0]] + (both[x.shape[0] :] + rest)
 
 
-def half_scratch():
-    block = lambda *lead: pltpu.VMEM((*lead, HALF, TILE), F32)
+def block_scratch():
+    block = lambda *lead: pltpu.VMEM((*lead, VEC, TILE), F32)
     return dict(
         far=block(N_ROW),
         near=block(N_COL),
@@ -81,16 +81,14 @@
 
 
 def own_scratch():
-    sums = lambda: pltpu.VMEM((SLOTS + 1, HALF, TILE), F32)
+    sums = lambda: pltpu.VMEM((SLOTS + 1, VEC, TILE), F32)
     return dict(
         table=pltpu.SMEM((T_SIZE,), jnp.int32),
         tiles_in=pltpu.VMEM((SLOTS, TILE, TILE), F32),
         high=pltpu.VMEM((SLOTS, TILE, TILE), BF16),
         low=pltpu.VMEM((SLOTS, TILE, TILE), BF16),
-        sum_far0=sums(),
-        sum_far1=sums(),
-        sum_near0=sums(),
-        sum_near1=sums(),
+        sum_far=sums(),
+        sum_near=sums(),
         upper=pltpu.VMEM((VEC, VEC), F32),
         inverse=pltpu.VMEM((VEC, VEC), F32),
         tile_sem=pltpu.SemaphoreType.DMA,
@@ -143,6 +141,7 @@
         r=r, z=z, s=s, x=x, y=y, p1=p1, p2=p2, slot=slot,
         r1p=dev(p1 + 1, p2), r1m=dev(p1 + 3, p2),
         r2p=dev(p1, p2 + 1), r2m=dev(p1, p2 + 3),
+        r1far=dev(p1 + 2, p2), r2far=dev(p1, p2 + 2),
         sib=(r + 1 - 2 * s, z),
         zp=(r, (z + 1) % N_COL), zm=(r, (z + N_COL - 1) % N_COL),
         z_peer=lambda d: (r, (z + d) % N_COL),
@@ -164,7 +163,11 @@
     pl.semaphore_wait(barrier, len(peers))
 
 
-def gather_steps(h, me, net, buf):
+def piece(j):
+    return pl.ds(j * (VEC // PIECES), VEC // PIECES)
+
+
+def gather_steps(me, net, buf, near_done):
     far, near = buf.far, buf.near
     p1, p2, z, slot = me.p1, me.p2, me.z, me.slot
     sib, r2, across = [], [], []
@@ -176,19 +179,20 @@
     def share(block):
         sib.append(send(block, me.sib))
 
-    def z_send(block, device):
-        ref = near.at[block % N_COL]
+    def z_send(block, j, device):
+        ref = near.at[block % N_COL, piece(j)]
         return net.copy(ref, ref, device)
 
     def z_step(d):
-        if d < 4 or h == 0:
-            zs["p", d].wait_recv()
-            if d < 3 or (d == 3 and h == 0):
-                zs["p", d + 1] = z_send(z + N_COL - d, me.zp)
-        if d < 4 or h == 1:
-            zs["m", d].wait_recv()
-            if d < 3 or (d == 3 and h == 1):
-                zs["m", d + 1] = z_send(z + d, me.zm)
+        for j in range(PIECES):
+            if d < 4 or j == 0:
+                zs["p", d, j].wait_recv()
+                if d < 3 or (d == 3 and j == 0):
+                    zs["p", d + 1, j] = z_send(z + N_COL - d, j, me.zp)
+            if d < 4 or j == 1:
+                zs["m", d, j].wait_recv()
+                if d < 3 or (d == 3 and j == 1):
+                    zs["m", d + 1, j] = z_send(z + d, j, me.zm)
 
     def column(block):
         r2.append((send(block, me.r2p), send(block, me.r2m)))
@@ -196,29 +200,28 @@
 
     def ring2(i, q1):
         up, down = r2[i]
+        on = far_column if i == 3 else None
         up.wait_recv()
-        if h == 0:
+        if i % 2 == 0 and on is None:
             on = send(slot(q1, p2 + 3), me.r2p)
         share(slot(q1, p2 + 3))
         down.wait_recv()
-        if h == 1:
+        if i % 2 == 1 and on is None:
             on = send(slot(q1, p2 + 1), me.r2m)
         share(slot(q1, p2 + 1))
         across.append((on, slot(q1, p2 + 2)))
 
     own = slot(p1, p2)
     r1 = [send(own, me.r1p), send(own, me.r1m)]
-    zs["p", 1] = z_send(z, me.zp)
-    zs["m", 1] = z_send(z, me.zm)
+    for j in range(PIECES):
+        zs["p", 1, j] = z_send(z, j, me.zp)
+        zs["m", 1, j] = z_send(z, j, me.zm)
     column(own)
+    on = send(own, me.r1far)
     yield
     r1[0].wait_recv()
-    if h == 0:
-        on = send(slot(p1 + 3, p2), me.r1p)
     column(slot(p1 + 3, p2))
     r1[1].wait_recv()
-    if h == 1:
-        on = send(slot(p1 + 1, p2), me.r1m)
     column(slot(p1 + 1, p2))
     yield
     z_step(1)
@@ -227,6 +230,7 @@
     yield
     on.wait_recv()
     column(slot(p1 + 2, p2))
+    far_column = send(slot(p1 + 2, p2), me.r2far)
     yield
     z_step(2)
     yield
@@ -238,12 +242,12 @@
     yield
     ring2(3, p1 + 2)
     yield
-    for i, (one, block) in enumerate(across):
+    z_step(4)
+    near_done()
+    yield
+    for one, block in across:
         one.wait_recv()
         share(block)
-        if i % 2:
-            yield
-    z_step(4)
     yield
     for one in sib:
         one.wait_recv()
@@ -265,12 +269,10 @@
         sum_near[k + 1] = res + sum_near[own.table[T_PREV_NEAR + k]]
 
 
-def reduce_steps(h, me, net, rows, own, buf, result):
-    p1, p2, z, s = me.p1, me.p2, me.z, me.s
-    total, pack, nears, tab = buf.total, buf.pack, buf.nears, own.table
-    sum_far = (own.sum_far0, own.sum_far1)[h]
-    sum_near = (own.sum_near0, own.sum_near1)[h]
-
+def mirror_part(me, net, rows, own, buf):
+    p1, s = me.p1, me.s
+    pack, tab = buf.pack, own.table
+    sum_far = own.sum_far
     mirror_products(rows, own, buf, sum_far)
     sib = []
     for q2 in (p1 + 2, p1 + 1, p1 + 3, p1):
@@ -280,32 +282,32 @@
         sib.append(
             net.copy(pack.at[pl.ds(base, SIDE)], buf.sib.at[pl.ds(base, SIDE)], me.sib)
         )
-    yield
-    upper_products(own, buf, sum_near)
-    for a in range(N_COL):
-        nears[a] = sum_near[tab[T_LAST_NEAR + a]]
+    return sib
+
+
+def reduce_steps(me, net, own, buf, sib, result):
+    p1, p2, z, s = me.p1, me.p2, me.z, me.s
+    total, nears, tab = buf.total, buf.nears, own.table
+    sum_far = own.sum_far
+    sum_near = own.sum_near
     zs = {}
     order1 = (p1 + 2, p1 + 1, p1 + 3, p1)
 
     def z_block(sign, d):
         return (z + d) % N_COL if sign == "p" else (z + N_COL - d) % N_COL
 
-    def z_send(sign, d):
-        zs[sign, d] = net.copy(
-            nears.at[z_block(sign, d)],
-            buf.zin.at[0 if sign == "p" else 1, d - 1],
-            me.zp if sign == "p" else me.zm,
-        )
-
-    def z_add(sign, d):
-        if (sign, d + 1) in zs:
-            zs[sign, d + 1].wait_recv()
-            nears[z_block(sign, d)] += buf.zin[0 if sign == "p" else 1, d]
-
-    def z_step(d):
-        for sign in "pm":
-            z_add(sign, d)
-            z_send(sign, d)
+    def z_step(d, parts=(("p", 0), ("m", 0), ("p", 1), ("m", 1))):
+        for sign, j in parts:
+            way = 0 if sign == "p" else 1
+            if (sign, d + 1, j) in zs:
+                zs[sign, d + 1, j].wait_recv()
+                nears[z_block(sign, d), piece(j)] += buf.zin[way, d, piece(j)]
+            if d:
+                zs[sign, d, j] = net.copy(
+                    nears.at[z_block(sign, d), piece(j)],
+                    buf.zin.at[way, d - 1, piece(j)],
+                    (me.zp, me.zm)[way],
+                )
 
     def at(q1, q2):
         return (q2 % SIDE) * SIDE + q1 % SIDE
@@ -316,33 +318,37 @@
             b = at(q1, q2)
             total[b] = sum_far[tab[T_LAST_FAR + s * 16 + b]] + buf.sib[b]
 
-    z_send("pm"[h], 4)
-    z_send("mp"[h], 3)
     whole(0, p2 + 2)
+    r2 = (me.r2p, me.r2m)
     ahead = [
-        net.copy(total.at[at(q1, p2 + 2)], buf.ring2a.at[i], (me.r2p, me.r2m)[h])
+        net.copy(total.at[at(q1, p2 + 2)], buf.ring2a.at[i], r2[i % 2])
         for i, q1 in enumerate(order1)
     ]
-    plain, summed = ((p2 + 3, p2 + 1), (p2 + 1, p2 + 3))[h]
-    whole((2, 1)[h], plain)
+    whole(1, p2 + 1)
+    whole(2, p2 + 3)
+    beside = (p2 + 1, p2 + 3)
     plain_copies = [
-        net.copy(total.at[at(q1, plain)], buf.ring2b.at[1 - h, i], (me.r2m, me.r2p)[h])
+        net.copy(
+            total.at[at(q1, beside[1 - i % 2])], buf.ring2b.at[1 - i % 2, i], r2[1 - i % 2]
+        )
         for i, q1 in enumerate(order1)
     ]
-    whole((1, 2)[h], summed)
-    yield
-    sign = "pm"[h]
-    z_add(sign, 3)
-    z_send(sign, 3)
+    yield
+    upper_products(own, buf, sum_near)
+    for a in range(N_COL):
+        nears[a] = sum_near[tab[T_LAST_NEAR + a]]
+    z_step(4, (("p", 0), ("m", 1)))
+    z_step(3, (("m", 0), ("p", 1)))
     yield
     summed_copies = []
     for i, q1 in enumerate(order1):
         ahead[i].wait_recv()
-        b = at(q1, summed)
+        b = at(q1, beside[i % 2])
         total[b] += buf.ring2a[i]
-        summed_copies.append(net.copy(total.at[b], buf.ring2b.at[h, i], (me.r2p, me.r2m)[h]))
+        summed_copies.append(net.copy(total.at[b], buf.ring2b.at[i % 2, i], r2[i % 2]))
         if i == 1:
             yield
+    z_step(3, (("p", 0), ("m", 1)))
     whole(3, p2)
     yield
     z_step(2)
@@ -355,39 +361,40 @@
         col[i] = total[at(order1[i], p2)] + (buf.ring2b[0, i] + buf.ring2b[1, i])
 
     gathered(0)
-    on = net.copy(col.at[0], buf.ring1a.at[0], (me.r1p, me.r1m)[h])
-    yield
-    gathered(2 - h)
-    b1 = net.copy(col.at[2 - h], buf.ring1b.at[1 - h], (me.r1m, me.r1p)[h])
+    on = net.copy(col.at[0], buf.ring1a.at[0], me.r1far)
+    yield
+    gathered(1)
+    b1 = net.copy(col.at[1], buf.ring1b.at[0], me.r1p)
     yield
     z_step(1)
     yield
-    gathered(1 + h)
-    on.wait_recv()
-    col[1 + h] += buf.ring1a[0]
-    b2 = net.copy(col.at[1 + h], buf.ring1b.at[h], (me.r1p, me.r1m)[h])
+    gathered(2)
+    b2 = net.copy(col.at[2], buf.ring1b.at[1], me.r1m)
     gathered(3)
     yield
-    z_add("p", 0)
-    z_add("m", 0)
+    z_step(0)
     part = col[3] + nears[z]
     yield
     b1.wait_recv()
     b2.wait_recv()
-    part = part + (buf.ring1b[0] + buf.ring1b[1])
-    result[HALF * h : HALF * (h + 1), :] = part
-
-
-def pipe_steps(h, me, net, rows, own, bufs, grams, first):
+    on.wait_recv()
+    result[...] = part + (buf.ring1b[0] + buf.ring1b[1]) + buf.ring1a[0]
+
+
+def pipe_steps(me, net, rows, own, bufs, grams, image):
     for it in range(ITERS):
-        buf = bufs[it][h]
-        image = first if it == 0 else grams[it - 1].image[HALF * h : HALF * (h + 1), :]
+        buf = bufs[it]
         buf.far[me.slot(me.p1, me.p2)] = image
         buf.near[me.z] = image
-        yield from gather_steps(h, me, net, buf)
-        yield
-        yield from reduce_steps(h, me, net, rows, own, buf, grams[it].image)
-        yield ("done", it)
+        sib = []
+
+        def near_done():
+            sib.extend(mirror_part(me, net, rows, own, buf))
+
+        yield from gather_steps(me, net, buf, near_done)
+        yield from reduce_steps(me, net, own, buf, sib, grams[it].image)
+        image = grams[it].image[...]
+        yield it
 
 
 def gram_steps(me, net, own, buf, image):
@@ -517,37 +524,29 @@
 
 
 def kernel(names, rows, cols, count, start, tiles, basis, factor, *scratch):
-    own_names, gram_names, half_names = names
+    own_names, gram_names, block_names = names
     refs = iter(scratch)
     take = lambda keys: SimpleNamespace(**{key: next(refs) for key in keys})
     own = take(own_names)
     grams = [take(gram_names) for _ in range(ITERS)]
-    bufs = [[take(half_names) for _ in range(2)] for _ in range(ITERS)]
+    bufs = [take(block_names) for _ in range(ITERS)]
     me = place()
     loading = pltpu.make_async_copy(tiles, own.tiles_in, own.tile_sem)
     loading.start()
     image = start[...].T
-    for ref in (own.sum_far0, own.sum_far1, own.sum_near0, own.sum_near1):
-        ref[0] = jnp.zeros((HALF, TILE), F32)
+    for ref in (own.sum_far, own.sum_near):
+        ref[0] = jnp.zeros((VEC, TILE), F32)
     enter(me)
 
     net = Net(own.send, own.recv)
-    pipes = [
-        pipe_steps(h, me, net, rows, own, bufs, grams, image[HALF * h : HALF * (h + 1)])
-        for h in range(2)
-    ]
     beside = prepare_steps(rows, cols, count, own, loading)
-    done = [None, None]
-    tick = 0
-    while any(d != ("done", ITERS - 1) for d in done):
-        for h in range(2):
-            if h == 0 or tick >= LAG:
-                at = next(pipes[h], None)
-                if at is not None:
-                    done[h] = at
-                    if at == ("done", 0) and done[1 - h] == ("done", 0):
-                        beside = gram_steps(me, net, own, grams[0], grams[0].image[...])
-        next(beside, None)
+    tick, every = 0, 1
+    for at in pipe_steps(me, net, rows, own, bufs, grams, image):
+        if at == 0:
+            beside = gram_steps(me, net, own, grams[0], grams[0].image[...])
+            tick, every = 0, EVERY
+        if tick % every == 0:
+            next(beside, None)
         tick += 1
     for _ in beside:
         pass
@@ -562,8 +561,8 @@
 
 
 def shards(start, tiles, tile_rows, tile_cols, tile_count):
-    own, gram, half = own_scratch(), gram_scratch(), half_scratch()
-    names = (tuple(own), tuple(gram), tuple(half))
+    own, gram, block = own_scratch(), gram_scratch(), block_scratch()
+    names = (tuple(own), tuple(gram), tuple(block))
     vmem = pl.BlockSpec(memory_space=pltpu.VMEM)
     smem = pl.BlockSpec(memory_space=pltpu.SMEM)
 
@@ -581,7 +580,7 @@
         scratch_shapes=[
             *own.values(),
             *(ref for _ in range(ITERS) for ref in gram.values()),
-            *(ref for _ in range(2 * ITERS) for ref in half.values()),
+            *(ref for _ in range(ITERS) for ref in block.values()),
         ],
         compiler_params=pltpu.CompilerParams(
             collective_id=0, has_side_effects=True, vmem_limit_bytes=62 * 1024 * 1024

time: 137 us -> 129 us (0.942)
  Pallas kernels: 132 us -> 124 us
    pallas_call x1, Pallas kernels: 132 us -> 124 us  [shards(): pl.pallas_call(body, out_shape=(jax.ShapeDtypeStruct((TILE, VEC), F32), j...]
where the time goes in v3:
time: 129 us
  Pallas kernels  124 us (96%)
  local copies, waits for them, and re-layouts  3.04 us (2%)
  between operations  1.29 us (1%)
    pallas_call x1, Pallas kernels, shards(): pl.pallas_call(body, out_shape=(jax.ShapeDtypeStruct((TILE, VEC), F32), j...  124 us
    unnamed x2, local copies, waits for them, and re-layouts  3.04 us

profile of v3, /device:TPU:1, one launch (start us, length us, event | category | flops | bytes accessed | tf_op | source)
XLA Modules:
  0.0 128.8 jit_solution(1515708469205982370)
XLA Ops:
  1.3 124.4 %shard_map.68 = (f32[256,128]{1,0:T(8,128)}, f32[128,128]{1,0:T(8,128)}) custom-call(s32[1,24]{1,0:T(1,128)} %refs_0_.1, s32[1,24]{1,0:T(1,128)} %refs_1_.1, s32[1]{0:T(128)S(6)} %copy.9.refs_2_, f32[256,128]{1,0:T(8,128)} %refs_3_.1, f32[24,256,256]{2,1,0:T(8,128)} %bitcast.1), custom_call_target="tpu_custom_call" | custom-call | tf_op jit(solution)/shard_map/pallas_call | solution.py:572
  125.7 1.6 %copy.10 = f32[256,128]{1,0:T(8,128)} copy(f32[256,128]{1,0:T(8,128)} %get-tuple-element.4) | data formatting | bytes 262144
  127.3 1.5 %copy.11 = f32[128,128]{1,0:T(8,128)} copy(f32[128,128]{1,0:T(8,128)} %get-tuple-element.5) | data formatting | bytes 131072
